TPU v7x, 32 devices: a whole 2x2x4 slice. The times are simulated.
32 devices in a mesh: parts: 1, tm: 32 (over z, y, x, core).
Axes of the slice: x: 2, y: 2, z: 4, core: 2. Of those that a mesh axis runs over, the one named last changes fastest.
Arguments:
- traces: bfloat16 [64, 1151], P(('parts', 'tm')), may hold values from -6 to 6
- templates: bfloat16 [64, 64, 128], P('tm'), may hold values from -0.5 to 0.5
- station_of_slot: int32 [64], replicated, may hold values from 0 to 63, each once
- travel_offsets: int32 [64, 2], replicated, may hold values from 0 to 15
- stack_weights: bfloat16 [2, 128, 64], replicated, may hold values from -6 to 6
Outputs:
- peak_stack: float32 [64, 1024], P('parts', 'tm')
Inputs may be any that keep to these rules, and one draw needn't show every extreme that they name: `station_of_slot`: each station stands in exactly one slot. `travel_offsets`: the greatest move-out is reached.
All inputs are finite; a program needn't handle non-finite values.
Results may differ from a plain program's by a relative error of at most 0.0011.
Values may be sent and summed in bfloat16 or wider, within the bound.
No kernel may reach another device: no remote copies, remote signals or barrier semaphores. Data moves between devices by JAX's collectives and lax.ppermute only.
A program may use at most 64 MiB of HBM per device.

v0:
```python
import jax
import jax.numpy as jnp
from jax import lax
from jax.sharding import PartitionSpec as P

MAXOFF = 16
NB = 2


def shifted_2(block, axis, distance):
    devices = range(lax.axis_size(axis))
    route = [(i - distance, i) for i in devices if i - distance in devices]
    return lax.ppermute(block, axis, route)


def correlate(rows, waveforms):
    row_count = rows.shape[0]
    tmpl_count = waveforms.shape[1]
    tmpl_len = waveforms.shape[2]
    kernel = waveforms.reshape(row_count * tmpl_count, 1, tmpl_len)
    raw_corr = lax.conv_general_dilated(
        rows[None],
        kernel,
        (1,),
        "VALID",
        dimension_numbers=("NCH", "OIH", "NCH"),
        feature_group_count=row_count,
        preferred_element_type=jnp.float32,
    )[0]
    raw_corr = raw_corr.reshape(row_count, tmpl_count, -1)
    out_len = raw_corr.shape[2]
    squared = rows.astype(jnp.float32)
    squared = squared * squared
    running = jnp.cumsum(
        jnp.concatenate([jnp.zeros((row_count, 1), jnp.float32), squared], axis=1), axis=1
    )
    energy = (running[:, tmpl_len : tmpl_len + out_len] - running[:, :out_len]) / tmpl_len
    return (raw_corr / jnp.sqrt(tmpl_len * (energy[:, None, :] + 1e-05))).astype(jnp.bfloat16)


def on_device(traces, templates, station_of_slot, travel_offsets, stack_weights):
    ncc = correlate(traces, templates)
    groups = lax.axis_size("tm")
    local_rows, tmpl_count, total_len = ncc.shape
    slab_len = total_len // groups
    outgoing = (
        ncc.reshape(local_rows, tmpl_count, groups, slab_len)
        .transpose(2, 0, 1, 3)
        .reshape(groups, local_rows, tmpl_count * slab_len)
    )
    received = lax.all_to_all(outgoing, "tm", split_axis=0, concat_axis=0, tiled=True).reshape(
        groups * local_rows, tmpl_count, slab_len
    )
    following = shifted_2(received[:, :, :MAXOFF], "tm", -1)
    extended = jnp.concatenate([received, following], axis=2)
    station_rows = extended.shape[0]
    slot_weights = stack_weights[:, :, station_of_slot]
    slot_offsets = travel_offsets[station_of_slot]

    def one_block(running, block_id):
        shifted = jax.vmap(
            lambda row_trace, shift_by: lax.dynamic_slice_in_dim(
                row_trace, shift_by, slab_len, axis=1
            )
        )(extended, slot_offsets[:, block_id])
        stacked = jnp.dot(
            slot_weights[block_id],
            shifted.reshape(station_rows, tmpl_count * slab_len),
            preferred_element_type=jnp.float32,
        )
        return (jnp.maximum(running, jnp.max(stacked, axis=0)), None)

    start = jnp.full((tmpl_count * slab_len,), -jnp.inf, jnp.float32)
    running, unused = lax.scan(one_block, start, jnp.arange(NB, dtype=jnp.int32))
    return running.reshape(tmpl_count, slab_len)


def solution(mesh):
    return jax.shard_map(
        on_device,
        mesh=mesh,
        in_specs=(P(("parts", "tm"), None), P("tm", None, None), P(), P(), P()),
        out_specs=P("parts", "tm"),
        check_vma=False,
    )
```

profile of v0, /device:TPU:1, one launch (start us, length us, event | category | flops | bytes accessed | tf_op | source)
XLA Modules:
  0.0 53.4 jit_solution(13268748483952977169)
XLA Ops:
  0.0 0.7 %convert_multiply_fusion = f32[2,1151]{1,0:T(2,128)S(1)} fusion(bf16[2,1151]{1,0:T(2,128)(2,1)} %param.7), kind=kLoop, calls=%fused_computation.29 | loop fusion | flops 4604 | bytes 13812 | tf_op jit(solution)/shard_map/mul | solution.py:33
  0.7 0.7 %pad.2 = bf16[2,1,1152]{2,0,1:T(2,128)(2,1)S(1)} pad(bf16[2,1,1151]{2,0,1:T(2,128)(2,1)} %bitcast.51, bf16[]{:T(256)} %constant.13.clone.1), padding=0_0x0_0x0_1 | pad | bytes 9214 | tf_op jit(solution)/shard_map/broadcast_in_dim | solution.py:22
  1.8 0.9 %copy.41 = bf16[128,128]{0,1:T(8,128)(2,1)S(1)} copy(bf16[128,128]{1,0:T(8,128)(2,1)} %bitcast.50) | data formatting | bytes 65536 | tf_op jit(solution)/shard_map/reshape
  2.6 3.8 %convolution_select_fusion = f32[8,144,128]{2,0,1:T(8,128)S(1)} fusion(pred[8,144]{0,1:T(8,128)(4,1)} %constant.48, bf16[2,1,7,127]{2,0,3,1:T(2,128)(2,1)S(1)} %slice.31, bf16[2,1,8,144]{2,0,3,1:T(2,128)(2,1)S(1)} %copy.40, s32[128]{0:T(128)} %constant.24.clone.1, bf16[128,128]{0,1:T(8,128)(2,1)S(1)} %copy.41), kind=kOutput, calls=%fused_computation.14 | convolution fusion | flops 75736480 | bytes 632420 | tf_op jit(solution)/shard_map/conv_general_dilated | solution.py:21
  6.6 0.6 %reshape_squeeze.3 = f32[2,64,32,32]{1,0,3,2:T(2,128)S(1)} reshape(f32[1,128,1024]{1,2,0:T(8,128)S(1)} %slice_bitcast_fusion) | data formatting | bytes 1048576 | tf_op jit(solution)/shard_map/reshape;squeeze | solution.py:30
  7.2 0.8 %copy.43 = f32[2,64,32,32]{3,1,2,0:T(8,128)S(1)} copy(f32[2,64,32,32]{1,0,3,2:T(2,128)S(1)} %reshape_squeeze.3) | data formatting | bytes 1048576 | tf_op jit(solution)/shard_map/reshape;squeeze | solution.py:30
  8.1 0.6 %reduce-window.6 = f32[2,9,128]{2,1,0:T(8,128)S(1)} reduce-window(f32[2,9,128]{2,1,0:T(8,128)S(1)} %reshape.36, f32[]{:T(128)} %constant.34.clone.1), window={size=1x1x128 pad=0_0x0_0x127_0}, to_apply=%region_0.0 | reduce-window | flops 292608 | bytes 18436 | tf_op jit(solution)/shard_map/reduce-window
  9.6 1.1 %reshape.38 = bf16[32,2,2048]{2,0,1:T(8,128)(2,1)S(1)} reshape(bf16[32,2,64,32]{3,2,0,1:T(8,128)(2,1)S(1)} %fusion.7) | data formatting | bytes 524288 | tf_op jit(solution)/shard_map/reshape | solution.py:49
  11.0 17.2 %all_to_all.5 = bf16[32,2,2048]{2,1,0:T(2,128)(2,1)S(1)} all-to-all(bf16[32,2,2048]{2,1,0:T(2,128)(2,1)S(1)} %copy.44), channel_id=1, replica_groups=mesh['parts'=1,'tm'=32] {'tm'}, dimensions={0} | all-to-all | bytes 524288 | tf_op jit(solution)/shard_map/all_to_all | solution.py:51
  28.1 0.5 reshape.39
  29.0 2.7 %collective-permute-start = (bf16[64,64,16]{1,2,0:T(8,128)(2,1)S(1)}, bf16[64,64,16]{1,2,0:T(8,128)(2,1)S(1)}, u32[]{:S(2)}, u32[]{:S(2)}) collective-permute-start(bf16[64,64,16]{1,2,0:T(8,128)(2,1)S(1)} %copy.45), channel_id=1, source_target_pairs={{1,0},{2,1},{3,2},{4,3},{5,4},{6,5},{7,6},{8,7},{9,8},{10,9},{11,1... | collective-permute-start | bytes 393224 | tf_op jit(solution)/shard_map/ppermute | solution.py:13
  31.9 0.6 %gather_fusion.2 = s32[64,2]{1,0:T(8,128)S(1)} fusion(s32[64,2]{1,0:T(8,128)S(1)} %copy.38, s32[1024]{0:T(1024)S(1)} %pad_clamp_fusion), kind=kCustom, calls=%fused_computation.2 | custom fusion | bytes 1280 | tf_op jit(solution)/shard_map/gather | solution.py:58
  32.5 0.7 %gather_fusion.1 = bf16[64,2,128]{2,0,1:T(8,128)(2,1)S(1)} fusion(bf16[2,128,64]{1,2,0:T(8,128)(2,1)S(1)} %copy-done, s32[1024]{0:T(1024)S(1)} %pad_clamp_fusion), kind=kCustom, calls=%fused_computation.1 | custom fusion | bytes 65792 | tf_op jit(solution)/shard_map/gather | solution.py:57
  33.3 3.4 %collective-permute-done = bf16[64,64,16]{1,2,0:T(8,128)(2,1)S(1)} collective-permute-done((bf16[64,64,16]{1,2,0:T(8,128)(2,1)S(1)}, bf16[64,64,16]{1,2,0:T(8,128)(2,1)S(1)}, u32[]{:S(2)}, u32[]{:S(2)}) %collective-permute-start) | collective-permute-done | bytes 131104 | tf_op jit(solution)/shard_map/ppermute | solution.py:13
  37.2 0.6 %pad_maximum_fusion = bf16[64,64,48]{2,1,0:T(8,128)(2,1)S(1)} fusion(bf16[64,64,16]{2,1,0:T(8,128)(2,1)S(1)} %copy.46, bf16[64,64,32]{2,1,0:T(8,128)(2,1)S(1)} %reshape.39), kind=kLoop, calls=%fused_computation.15 | loop fusion | flops 786432 | bytes 786432 | tf_op jit(solution)/shard_map/concatenate | solution.py:55
  37.8 1.3 %copy.49 = bf16[64,64,48]{1,0,2:T(8,128)(2,1)S(1)} copy(bf16[64,64,48]{2,1,0:T(8,128)(2,1)S(1)} %pad_maximum_fusion) | data formatting | bytes 786432
  39.1 13.6 %while.11 = (s32[]{:T(128)}, f32[2048]{0:T(1024)S(1)}, s32[2]{0:T(128)S(1)}, bf16[2,128,64]{1,2,0:T(8,128)(2,1)S(1)}, s32[64,2]{0,1:T(2,128)S(1)}, /*index=5*/bf...) while((s32[]{:T(128)}, f32[2048]{0:T(1024)S(1)}, s32[2]{0:T(128)S(1)}, ...), condition=%wide.region_4.5_spmd.clone, body=%wide.region_2.4_spmd.clone.sunk | while | flops 33819140 | bytes 1623453 | solution.py:74
  39.1 0.7 %dynamic_slice.23 = s32[1]{0:T(128)} dynamic-slice(s32[2]{0:T(128)S(1)} %get-tuple-element.152, s32[]{:T(128)} %get-tuple-element.141), dynamic_slice_sizes={1} | dynamic-slice | bytes 12 | tf_op jit(solution)/shard_map/while/body/jit(dynamic_index_in_dim)/dynamic_slice | solution.py:74
  41.9 2.9 %gather_fusion = bf16[64,64,32]{1,0,2:T(8,128)(2,1)S(1)} fusion(bf16[64,64,48]{1,0,2:T(8,128)(2,1)S(1)} %get-tuple-element.155, s32[64]{0:T(128)S(1)} %fusion.28), kind=kCustom, calls=%fused_computation.clone.clone.1 | custom fusion | bytes 525056 | tf_op jit(solution)/shard_map/while/body/eval_jaxpr/vmap()/gather | solution.py:62
  44.7 0.8 %copy.56 = bf16[64,64,32]{0,2,1:T(8,128)(2,1)S(1)} copy(bf16[64,64,32]{1,0,2:T(8,128)(2,1)S(1)} %gather_fusion) | data formatting | bytes 524288 | tf_op jit(solution)/shard_map/while/body/eval_jaxpr/vmap()/gather | solution.py:62
  45.9 0.7 %dynamic_slice.23 = s32[1]{0:T(128)} dynamic-slice(s32[2]{0:T(128)S(1)} %get-tuple-element.152, s32[]{:T(128)} %get-tuple-element.141), dynamic_slice_sizes={1} | dynamic-slice | bytes 12 | tf_op jit(solution)/shard_map/while/body/jit(dynamic_index_in_dim)/dynamic_slice | solution.py:74
  48.7 2.9 %gather_fusion = bf16[64,64,32]{1,0,2:T(8,128)(2,1)S(1)} fusion(bf16[64,64,48]{1,0,2:T(8,128)(2,1)S(1)} %get-tuple-element.155, s32[64]{0:T(128)S(1)} %fusion.28), kind=kCustom, calls=%fused_computation.clone.clone.1 | custom fusion | bytes 525056 | tf_op jit(solution)/shard_map/while/body/eval_jaxpr/vmap()/gather | solution.py:62
  51.5 0.8 %copy.56 = bf16[64,64,32]{0,2,1:T(8,128)(2,1)S(1)} copy(bf16[64,64,32]{1,0,2:T(8,128)(2,1)S(1)} %gather_fusion) | data formatting | bytes 524288 | tf_op jit(solution)/shard_map/while/body/eval_jaxpr/vmap()/gather | solution.py:62
  52.8 0.7 %copy.50 = f32[64,32]{0,1:T(8,128)} copy(f32[64,32]{1,0:T(8,128)S(1)} %reshape.40) | data formatting | bytes 16384 | tf_op jit(solution)/shard_map/reshape | solution.py:75
  (36 shorter events, 3.5 us)
Async XLA Ops:
  0.0 32.5 %copy-start = (bf16[2,128,64]{1,2,0:T(8,128)(2,1)S(1)}, bf16[2,128,64]{1,2,0:T(8,128)(2,1)}, u32[]{:S(2)}) copy-start(bf16[2,128,64]{1,2,0:T(8,128)(2,1)} %param.11) | copy-start | bytes 98308
  10.7 21.0 %copy-start.2 = (s32[64]{0:T(128)S(1)}, s32[64]{0:T(128)}, u32[]{:S(2)}) copy-start(s32[64]{0:T(128)} %param.9) | copy-start | bytes 772
  10.7 21.0 %copy-start.1 = (s32[64,2]{0,1:T(2,128)S(1)}, s32[64,2]{0,1:T(2,128)}, u32[]{:S(2)}) copy-start(s32[64,2]{0,1:T(2,128)} %param.10) | copy-start | bytes 1540
  29.0 7.7 %collective-permute-start = (bf16[64,64,16]{1,2,0:T(8,128)(2,1)S(1)}, bf16[64,64,16]{1,2,0:T(8,128)(2,1)S(1)}, u32[]{:S(2)}, u32[]{:S(2)}) collective-permute-start(bf16[64,64,16]{1,2,0:T(8,128)(2,1)S(1)} %copy.45), channel_id=1, source_target_pairs={{1,0},{2,1},{3,2},{4,3},{5,4},{6,5},{7,6},{8,7},{9,8},{10,9},{11,1... | collective-permute-start | bytes 393224 | tf_op jit(solution)/shard_map/ppermute | solution.py:13
where the time goes:
time: 53.9 us; the launch traced here: 53.4 us
  local copies, waits for them, and re-layouts  18.7 us (35%)
  blocking collectives  17.2 us (32%)
  matrix products  4.47 us (8%)
  loops' own time  4.26 us (8%)
  waiting for transfers between devices  3.44 us (6%)
  starting transfers between devices  2.68 us (5%)
  other arithmetic  2.49 us (5%)
    all_to_all x1, blocking collectives, on_device(): lax.all_to_all(outgoing, 'tm', split_axis=0, concat_axis=0, tiled=True)  17.2 us
    gather x4, local copies, waits for them, and re-layouts, one_block(): lax.dynamic_slice_in_dim(row_trace, shift_by, slab_len, axis=1)  7.27 us
    another operation x1, loops' own time, on_device(): lax.scan(one_block, start, jnp.arange(NB, dtype=jnp.int32))  4.26 us
    conv_general_dilated x1, matrix products, correlate(): lax.conv_general_dilated(rows[None], kernel, (1,), 'VALID', dimension_num...  3.78 us
    ppermute x1, waiting for transfers between devices, shifted_2(): return lax.ppermute(block, axis, route)  3.44 us
    ppermute x1, starting transfers between devices, shifted_2(): return lax.ppermute(block, axis, route)  2.68 us
    unnamed x10, local copies, waits for them, and re-layouts  1.5 us
    another operation x2, local copies, waits for them, and re-layouts, correlate(): raw_corr = raw_corr.reshape(row_count, tmpl_count, -1)  1.44 us
  transfers between devices with their start and end apart: 1, of which 1 were waited for; matrix products, arithmetic and copies ran while one was open for 3% of the time, Pallas kernels for 0%

commit v1 on v0

v1 whole, which is shorter than its diff:
```python
import jax
import jax.numpy as jnp
from jax import lax
from jax.experimental import pallas as pl
from jax.experimental.pallas import tpu as pltpu
from jax.sharding import PartitionSpec as P

MAXOFF = 16
LANES = 128
F32 = jnp.float32
BF16 = jnp.bfloat16
BY_LANES = (((1,), (1,)), ((), ()))
BY_ROWS = (((0,), (0,)), ((), ()))


def on_diagonal(blocks):
    zero = jnp.zeros_like(blocks[0])
    return jnp.concatenate(
        [
            jnp.concatenate([b if i == j else zero for j in range(len(blocks))], axis=1)
            for i, b in enumerate(blocks)
        ],
        axis=0,
    )


def correlate_kernel(slab, traces_ref, templates_ref, out_ref, samples):
    row_count, length = traces_ref.shape
    tmpl_len = templates_ref.shape[2]
    groups = out_ref.shape[0]
    per_tile = LANES // slab
    samples[...] = jnp.zeros_like(samples)
    samples[:, :length] = traces_ref[...].astype(F32)
    waveforms = on_diagonal([templates_ref[s] for s in range(row_count)])
    ones = on_diagonal([jnp.ones(templates_ref.shape[1:], BF16)] * row_count)
    out_ref[groups - 1, :MAXOFF] = jnp.zeros((MAXOFF, out_ref.shape[2]), BF16)
    for tile in range(groups * slab // LANES):
        windows = []
        for s in range(row_count):
            stretch = samples[s : s + 1, tile * LANES : tile * LANES + LANES + tmpl_len]
            stretch = jnp.broadcast_to(stretch, (LANES, LANES + tmpl_len))
            rolled = pltpu.roll(stretch, tmpl_len + 1, 1, stride=1, stride_axis=0)
            windows.append(rolled[:, :tmpl_len])
        window = jnp.concatenate(windows, axis=1)
        square = window * window
        high = square.astype(BF16)
        low = (square - high.astype(F32)).astype(BF16)
        raw = lax.dot_general(window.astype(BF16), waveforms, BY_LANES, preferred_element_type=F32)
        power = lax.dot_general(high, ones, BY_LANES, preferred_element_type=F32)
        power += lax.dot_general(low, ones, BY_LANES, preferred_element_type=F32)
        ncc = (raw * lax.rsqrt(power + tmpl_len * 1e-05)).astype(BF16)
        for part in range(per_tile):
            d = tile * per_tile + part
            mine = ncc[LANES - (part + 1) * slab : LANES - part * slab]
            out_ref[d, MAXOFF:] = mine
            if d > 0:
                out_ref[d - 1, :MAXOFF] = mine[slab - MAXOFF :]


def weights_kernel(row_count, stations_ref, weights_ref, out_ref):
    slots = stations_ref.shape[1]
    first = lax.broadcasted_iota(jnp.int32, (slots, slots), 0)
    second = lax.broadcasted_iota(jnp.int32, (slots, slots), 1)
    groups = slots // row_count
    standing = (first == stations_ref[...]).astype(BF16)
    wanted = (first == (second % groups) * row_count + second // groups).astype(BF16)
    order = jnp.dot(standing, wanted, preferred_element_type=F32).astype(BF16)
    for b in range(weights_ref.shape[0]):
        out_ref[b] = lax.dot_general(
            weights_ref[b], order, BY_ROWS, preferred_element_type=F32
        ).astype(BF16)


def stack_kernel(
    slab, row_count, stations_ref, offsets_ref, weights_ref, parts_ref, out_ref, wide, moved
):
    groups, rows, lanes = parts_ref.shape
    blocks = weights_ref.shape[0]
    tmpl_count = lanes // row_count
    lane = lax.broadcasted_iota(jnp.int32, (slab, lanes), 1)

    def shift(src, unused):
        wide[...] = parts_ref[src].astype(F32)
        for b in range(blocks):
            moment = None
            for s in range(row_count):
                off = offsets_ref[b, stations_ref[src * row_count + s]]
                piece = wide[pl.ds(MAXOFF - off, slab), :]
                moment = piece if s == 0 else jnp.where(lane < s * tmpl_count, moment, piece)
            moved[b, pl.ds(src, slab, stride=groups), :] = moment
        return unused

    lax.fori_loop(0, groups, shift, 0, unroll=4)

    low_half = lax.broadcasted_iota(jnp.int32, (groups, lanes), 1) < tmpl_count
    times = 4
    for q in range(0, slab, times):
        best = None
        for b in range(blocks):
            columns = []
            for p in range(q, q + times, 2):
                even = moved[b, p * groups : (p + 1) * groups, :]
                odd = moved[b, (p + 1) * groups : (p + 2) * groups, :]
                top = jnp.where(low_half, even, pltpu.roll(odd, tmpl_count, 1))
                bottom = jnp.where(low_half, pltpu.roll(even, tmpl_count, 1), odd)
                columns.append(jnp.concatenate([top, bottom], axis=0).astype(BF16))
            stacked = jnp.dot(
                weights_ref[b], jnp.concatenate(columns, axis=1), preferred_element_type=F32
            )
            peak = jnp.max(stacked, axis=0, keepdims=True)
            best = peak if b == 0 else jnp.maximum(best, peak)
        for p in range(times):
            row = slab - 1 - q - p
            out_ref[row : row + 1, :] = best[:, p * tmpl_count : (p + 1) * tmpl_count]


def on_device(traces, templates, station_of_slot, travel_offsets, stack_weights):
    groups = lax.axis_size("tm")
    row_count, tmpl_count, tmpl_len = templates.shape
    slab = (traces.shape[1] - tmpl_len + 1) // groups
    slots = station_of_slot.shape[0]
    blocks, nodes, unused = stack_weights.shape
    lanes = row_count * tmpl_count
    vmem = pl.BlockSpec(memory_space=pltpu.VMEM)
    smem = pl.BlockSpec(memory_space=pltpu.SMEM)

    parts = pl.pallas_call(
        lambda *refs: correlate_kernel(slab, *refs),
        out_shape=jax.ShapeDtypeStruct((groups, slab + MAXOFF, lanes), BF16),
        in_specs=[vmem, vmem],
        out_specs=vmem,
        scratch_shapes=[pltpu.VMEM((row_count, groups * slab + LANES + tmpl_len), F32)],
        name="correlate",
    )(traces, templates)
    received = lax.all_to_all(parts, "tm", split_axis=0, concat_axis=0, tiled=True)
    weights = pl.pallas_call(
        lambda *refs: weights_kernel(row_count, *refs),
        out_shape=jax.ShapeDtypeStruct((blocks, nodes, slots), BF16),
        in_specs=[vmem, vmem],
        out_specs=vmem,
        name="order_weights",
    )(station_of_slot[None], jnp.swapaxes(stack_weights, 1, 2))
    peaks = pl.pallas_call(
        lambda *refs: stack_kernel(slab, row_count, *refs),
        out_shape=jax.ShapeDtypeStruct((slab, tmpl_count), F32),
        in_specs=[smem, smem, vmem, vmem],
        out_specs=vmem,
        scratch_shapes=[
            pltpu.VMEM((slab + MAXOFF, lanes), F32),
            pltpu.VMEM((blocks, slab * groups, lanes), F32),
        ],
        name="stack",
    )(station_of_slot, travel_offsets.T, weights, received)
    return peaks.T


def solution(mesh):
    return jax.shard_map(
        on_device,
        mesh=mesh,
        in_specs=(P(("parts", "tm"), None), P("tm", None, None), P(), P(), P()),
        out_specs=P("parts", "tm"),
        check_vma=False,
    )
```

time: 53.9 us -> 27.4 us (0.51)
  the two profiles are of different devices: /device:TPU:1 before, /device:TPU:0 now
where the time goes in v1:
time: 27.4 us; the launch traced here: 27 us
  waiting for transfers between devices  11.5 us (42%)
  Pallas kernels  7.48 us (27%)
  starting transfers between devices  7.3 us (27%)
  local copies, waits for them, and re-layouts  0.76 us (3%)
    all_to_all x1, waiting for transfers between devices, on_device(): lax.all_to_all(parts, 'tm', split_axis=0, concat_axis=0, tiled=True)  11.5 us
    all_to_all x1, starting transfers between devices, on_device(): lax.all_to_all(parts, 'tm', split_axis=0, concat_axis=0, tiled=True)  7.3 us
    pallas_call x1, Pallas kernels, on_device(): pl.pallas_call(lambda *refs: stack_kernel(slab, row_count, *refs), out_sh...  3.47 us
    pallas_call x1, Pallas kernels, on_device(): pl.pallas_call(lambda *refs: correlate_kernel(slab, *refs), out_shape=jax...  2.32 us
    pallas_call x1, Pallas kernels, on_device(): pl.pallas_call(lambda *refs: weights_kernel(row_count, *refs), out_shape=...  1.68 us
    unnamed x2, local copies, waits for them, and re-layouts  0.76 us
  transfers between devices with their start and end apart: 1, of which 1 were waited for; matrix products, arithmetic and copies ran while one was open for 0% of the time, Pallas kernels for 6%

profile of v1, /device:TPU:0, one launch (start us, length us, event | category | flops | bytes accessed | tf_op | source)
XLA Modules:
  0.0 27.0 jit_solution(12072382054907382210)
XLA Ops:
  0.0 2.3 %correlate.1 = bf16[32,48,128]{2,1,0:T(8,128)(2,1)} custom-call(bf16[2,1151]{1,0:T(2,128)(2,1)} %refs_0_.2, bf16[2,64,128]{2,1,0:T(8,128)(2,1)} %refs_1_.1), custom_call_target="tpu_custom_call" | custom-call | tf_op jit(solution)/shard_map/correlate/pallas_call | solution.py:127
  2.3 7.3 %all-to-all-start = ((bf16[32,48,128]{2,1,0:T(8,128)(2,1)}), bf16[32,48,128]{2,1,0:T(8,128)(2,1)S(1)}, u32[]{:S(2)}, u32[]{:S(2)}) async-start(bf16[32,48,128]{2,1,0:T(8,128)(2,1)} %correlate.1), calls=%async_computation | async-start | bytes 786432 | tf_op jit(solution)/shard_map/all_to_all | solution.py:135
  9.6 1.7 %order_weights.1.refs_2_ = bf16[2,128,64]{2,1,0:T(8,128)(2,1)} custom-call(s32[1,64]{1,0:T(1,128)} %bitcast.5, bf16[2,64,128]{2,1,0:T(8,128)(2,1)} %bitcast.4), custom_call_target="tpu_custom_call" | custom-call | tf_op jit(solution)/shard_map/order_weights/pallas_call | solution.py:136
  11.3 11.5 %all-to-all-done.refs_3_ = bf16[32,48,128]{2,1,0:T(8,128)(2,1)S(1)} async-done(((bf16[32,48,128]{2,1,0:T(8,128)(2,1)}), bf16[32,48,128]{2,1,0:T(8,128)(2,1)S(1)}, u32[]{:S(2)}, u32[]{:S(2)}) %all-to-all-start) | async-done | bytes 393248 | tf_op jit(solution)/shard_map/all_to_all | solution.py:135
  22.8 0.0 copy-start
  22.8 0.8 %copy-done = bf16[32,48,128]{2,1,0:T(8,128)(2,1)} copy-done((bf16[32,48,128]{2,1,0:T(8,128)(2,1)}, bf16[32,48,128]{2,1,0:T(8,128)(2,1)S(1)}, u32[]{:S(2)}) %copy-start) | copy-done | bytes 393240
  23.6 3.5 %stack.1 = f32[32,64]{1,0:T(8,128)} custom-call(s32[64]{0:T(128)} %refs_0_.3, s32[2,64]{1,0:T(2,128)} %bitcast.6, bf16[2,128,64]{2,1,0:T(8,128)(2,1)} %order_weights.1.refs_2_, bf16[32,48,128]{2,1,0:T(8,128)(2,1)} %copy-done), custom_call_target="tpu_custom_call" | custom-call | tf_op jit(solution)/shard_map/stack/pallas_call | solution.py:143
Async XLA Ops:
  2.3 20.5 %all-to-all-start = ((bf16[32,48,128]{2,1,0:T(8,128)(2,1)}), bf16[32,48,128]{2,1,0:T(8,128)(2,1)S(1)}, u32[]{:S(2)}, u32[]{:S(2)}) async-start(bf16[32,48,128]{2,1,0:T(8,128)(2,1)} %correlate.1), calls=%async_computation | async-start | bytes 786432 | tf_op jit(solution)/shard_map/all_to_all | solution.py:135
  22.8 0.8 %copy-start = (bf16[32,48,128]{2,1,0:T(8,128)(2,1)}, bf16[32,48,128]{2,1,0:T(8,128)(2,1)S(1)}, u32[]{:S(2)}) copy-start(bf16[32,48,128]{2,1,0:T(8,128)(2,1)S(1)} %all-to-all-done.refs_3_) | copy-start | bytes 1179652

commit v2 on v1

v2 whole, which is shorter than its diff:
```python
import jax
import jax.numpy as jnp
from jax import lax
from jax.experimental import pallas as pl
from jax.experimental.pallas import tpu as pltpu
from jax.sharding import PartitionSpec as P

MAXOFF = 16
LANES = 128
F32 = jnp.float32
BF16 = jnp.bfloat16
BY_LANES = (((1,), (1,)), ((), ()))
BY_ROWS = (((0,), (0,)), ((), ()))
PARAMS = pltpu.CompilerParams(vmem_limit_bytes=24 << 20)


def on_diagonal(blocks):
    zero = jnp.zeros_like(blocks[0])
    return jnp.concatenate(
        [
            jnp.concatenate([b if i == j else zero for j in range(len(blocks))], axis=1)
            for i, b in enumerate(blocks)
        ],
        axis=0,
    )


def slot_tables(row_count, stations_ref, offsets_ref, weights_ref, moves_ref, columns_ref):
    slots = stations_ref.shape[1]
    groups = slots // row_count
    first = lax.broadcasted_iota(jnp.int32, (slots, slots), 0)
    second = lax.broadcasted_iota(jnp.int32, (slots, slots), 1)
    standing = (first == stations_ref[...]).astype(BF16)
    wanted = (first == (second % groups) * row_count + second // groups).astype(BF16)
    order = jnp.dot(standing, wanted, preferred_element_type=F32).astype(BF16)
    moves = jnp.dot(offsets_ref[...].astype(BF16), order, preferred_element_type=F32)
    moves_ref[...] = moves.astype(jnp.int32)
    for b in range(weights_ref.shape[0]):
        columns = lax.dot_general(weights_ref[b], order, BY_ROWS, preferred_element_type=F32)
        columns_ref[b] = columns.astype(BF16)


def correlate_kernel(slab, *refs):
    sources, (out_ref, moves_ref, columns_ref) = refs[:5], refs[5:8]
    held, samples, sems = refs[8:13], refs[13], refs[14]
    copies = [pltpu.make_async_copy(a, b, sems.at[i]) for i, (a, b) in enumerate(zip(sources, held))]
    for copy in copies:
        copy.start()
    traces_ref, templates_ref = held[:2]
    row_count, length = traces_ref.shape
    tmpl_len = templates_ref.shape[2]
    groups = out_ref.shape[0]
    per_tile = LANES // slab
    samples[...] = jnp.zeros_like(samples)
    out_ref[groups - 1, :MAXOFF] = jnp.zeros((MAXOFF, out_ref.shape[2]), BF16)
    ones = on_diagonal([jnp.ones(templates_ref.shape[1:], BF16)] * row_count)
    for copy in copies:
        copy.wait()
    samples[:, :length] = traces_ref[...].astype(F32)
    waveforms = on_diagonal([templates_ref[s] for s in range(row_count)])
    for tile in range(groups * slab // LANES):
        windows = []
        for s in range(row_count):
            stretch = samples[s : s + 1, tile * LANES : tile * LANES + LANES + tmpl_len]
            stretch = jnp.broadcast_to(stretch, (LANES, LANES + tmpl_len))
            rolled = pltpu.roll(stretch, tmpl_len + 1, 1, stride=1, stride_axis=0)
            windows.append(rolled[:, :tmpl_len])
        window = jnp.concatenate(windows, axis=1)
        square = window * window
        high = square.astype(BF16)
        low = (square - high.astype(F32)).astype(BF16)
        raw = lax.dot_general(window.astype(BF16), waveforms, BY_LANES, preferred_element_type=F32)
        power = lax.dot_general(high, ones, BY_LANES, preferred_element_type=F32)
        power += lax.dot_general(low, ones, BY_LANES, preferred_element_type=F32)
        ncc = (raw * lax.rsqrt(power + tmpl_len * 1e-05)).astype(BF16)
        for part in range(per_tile):
            d = tile * per_tile + part
            mine = ncc[LANES - (part + 1) * slab : LANES - part * slab]
            out_ref[d, MAXOFF:] = mine
            if d > 0:
                out_ref[d - 1, :MAXOFF] = mine[slab - MAXOFF :]
    slot_tables(row_count, *held[2:], moves_ref, columns_ref)


def stack_kernel(slab, row_count, moves_ref, weights_ref, parts_ref, out_ref, wide, moved):
    groups, rows, lanes = parts_ref.shape
    blocks = weights_ref.shape[0]
    tmpl_count = lanes // row_count
    pitch = groups + 1
    lane = lax.broadcasted_iota(jnp.int32, (slab, lanes), 1)
    wide[...] = parts_ref[...].astype(F32)
    moves = moves_ref[...]
    for src in range(groups):
        for b in range(blocks):
            moment = None
            for s in range(row_count):
                start = MAXOFF - moves[b, s * groups + src]
                piece = wide[src, pl.ds(start, slab), :]
                moment = piece if s == 0 else jnp.where(lane < s * tmpl_count, moment, piece)
            moved[b, pl.ds(src, slab, stride=pitch), :] = moment

    low_half = lax.broadcasted_iota(jnp.int32, (groups, lanes), 1) < tmpl_count
    times = 4
    for q in range(0, slab, times):
        best = None
        for b in range(blocks):
            columns = []
            for p in range(q, q + times, 2):
                even = moved[b, p * pitch : p * pitch + groups, :]
                odd = moved[b, (p + 1) * pitch : (p + 1) * pitch + groups, :]
                top = jnp.where(low_half, even, pltpu.roll(odd, tmpl_count, 1))
                bottom = jnp.where(low_half, pltpu.roll(even, tmpl_count, 1), odd)
                columns.append(jnp.concatenate([top, bottom], axis=0).astype(BF16))
            stacked = jnp.dot(
                weights_ref[b], jnp.concatenate(columns, axis=1), preferred_element_type=F32
            )
            peak = jnp.max(stacked, axis=0, keepdims=True)
            best = peak if b == 0 else jnp.maximum(best, peak)
        for p in range(times):
            row = slab - 1 - q - p
            out_ref[row : row + 1, :] = best[:, p * tmpl_count : (p + 1) * tmpl_count]


def in_hbm(array):
    return pltpu.with_memory_space_constraint(array, pltpu.HBM)


def on_device(traces, templates, station_of_slot, travel_offsets, stack_weights):
    groups = lax.axis_size("tm")
    row_count, tmpl_count, tmpl_len = templates.shape
    slab = (traces.shape[1] - tmpl_len + 1) // groups
    slots = station_of_slot.shape[0]
    blocks, nodes, unused = stack_weights.shape
    lanes = row_count * tmpl_count
    vmem = pl.BlockSpec(memory_space=pltpu.VMEM)
    hbm = pl.BlockSpec(memory_space=pltpu.HBM)
    sources = (traces, templates, station_of_slot[None], travel_offsets.T, jnp.swapaxes(stack_weights, 1, 2))

    parts, moves, weights = pl.pallas_call(
        lambda *refs: correlate_kernel(slab, *refs),
        out_shape=(
            jax.ShapeDtypeStruct((groups, slab + MAXOFF, lanes), BF16),
            jax.ShapeDtypeStruct((blocks, slots), jnp.int32),
            jax.ShapeDtypeStruct((blocks, nodes, slots), BF16),
        ),
        in_specs=[hbm] * len(sources),
        out_specs=(vmem, vmem, vmem),
        scratch_shapes=[
            *(pltpu.VMEM(a.shape, a.dtype) for a in sources),
            pltpu.VMEM((row_count, groups * slab + LANES + tmpl_len), F32),
            pltpu.SemaphoreType.DMA((len(sources),)),
        ],
        compiler_params=PARAMS,
        name="correlate",
    )(*(in_hbm(a) for a in sources))
    received = lax.all_to_all(parts, "tm", split_axis=0, concat_axis=0, tiled=True)
    peaks = pl.pallas_call(
        lambda *refs: stack_kernel(slab, row_count, *refs),
        out_shape=jax.ShapeDtypeStruct((slab, tmpl_count), F32),
        in_specs=[vmem, vmem, vmem],
        out_specs=vmem,
        scratch_shapes=[
            pltpu.VMEM((groups, slab + MAXOFF, lanes), F32),
            pltpu.VMEM((blocks, slab * (groups + 1), lanes), F32),
        ],
        compiler_params=PARAMS,
        name="stack",
    )(moves, weights, received)
    return peaks.T


def solution(mesh):
    return jax.shard_map(
        on_device,
        mesh=mesh,
        in_specs=(P(("parts", "tm"), None), P("tm", None, None), P(), P(), P()),
        out_specs=P("parts", "tm"),
        check_vma=False,
    )
```

time: 27.4 us -> 23.7 us (0.86)
  blocking collectives: 0 us -> 20.3 us
  waiting for transfers between devices: 11.5 us -> 0 us
  starting transfers between devices: 7.3 us -> 0 us
  Pallas kernels: 7.48 us -> 3.23 us
  local copies, waits for them, and re-layouts: 0.76 us -> 0 us
    all_to_all x0 -> x1, blocking collectives: none -> 20.3 us  [on_device(): lax.all_to_all(parts, 'tm', split_axis=0, concat_axis=0, tiled=True)]
    all_to_all x1 -> x0, waiting for transfers between devices: 11.5 us -> none  [on_device(): lax.all_to_all(parts, 'tm', split_axis=0, concat_axis=0, tiled=True)]
    all_to_all x1 -> x0, starting transfers between devices: 7.3 us -> none  [on_device(): lax.all_to_all(parts, 'tm', split_axis=0, concat_axis=0, tiled=True)]
    pallas_call x2 -> x1, Pallas kernels: 4 us -> 1.77 us  [on_device(): pl.pallas_call(lambda *refs: correlate_kernel(slab, *refs), out_shape=(ja...]
    pallas_call x1, Pallas kernels: 3.47 us -> 1.46 us  [on_device(): pl.pallas_call(lambda *refs: stack_kernel(slab, row_count, *refs), out_sh...]
    unnamed x2 -> x0, local copies, waits for them, and re-layouts: 0.76 us -> none
  transfers between devices with their start and end apart: 1 -> 0, of which waited for: 1 -> 0; matrix products, arithmetic and copies ran while one was open for 0% -> 0% of each run, Pallas kernels for 6% -> 0%
where the time goes in v2:
time: 23.7 us; the launch traced here: 23.5 us
  blocking collectives  20.3 us (86%)
  Pallas kernels  3.23 us (14%)
    all_to_all x1, blocking collectives, on_device(): lax.all_to_all(parts, 'tm', split_axis=0, concat_axis=0, tiled=True)  20.3 us
    pallas_call x1, Pallas kernels, on_device(): pl.pallas_call(lambda *refs: correlate_kernel(slab, *refs), out_shape=(ja...  1.77 us
    pallas_call x1, Pallas kernels, on_device(): pl.pallas_call(lambda *refs: stack_kernel(slab, row_count, *refs), out_sh...  1.46 us

profile of v2, /device:TPU:0, one launch (start us, length us, event | category | flops | bytes accessed | tf_op | source)
XLA Modules:
  0.0 23.5 jit_solution(17913502336398348335)
XLA Ops:
  0.0 1.8 %correlate.1 = (bf16[32,48,128]{2,1,0:T(8,128)(2,1)S(1)}, s32[2,64]{1,0:T(2,128)S(1)}, bf16[2,128,64]{2,1,0:T(8,128)(2,1)S(1)}) custom-call(bf16[2,1151]{1,0:T(2,128)(2,1)} %refs_0_.1, bf16[2,64,128]{2,1,0:T(8,128)(2,1)} %refs_1_.1, s32[1,64]{1,0:T(1,128)} %bitcast.6, s32[2,64]{1,0:T(2,128)} %bitcast.5, bf16[2,64,128]{2,1,0:T(8,128)(2,1)} %bitcast.4), custom_call_target="tpu_custom_call" | custom-call | tf_op jit(solution)/shard_map/correlate/pallas_call | solution.py:139
  1.8 20.3 %all_to_all.5.refs_2_ = bf16[32,48,128]{2,1,0:T(8,128)(2,1)S(1)} all-to-all(bf16[32,48,128]{2,1,0:T(8,128)(2,1)S(1)} %get-tuple-element.10), channel_id=1, replica_groups=mesh['parts'=1,'tm'=32] {'tm'}, dimensions={0} | all-to-all | bytes 786432 | tf_op jit(solution)/shard_map/all_to_all | solution.py:156
  22.1 1.5 %stack.1 = f32[32,64]{1,0:T(8,128)} custom-call(s32[2,64]{1,0:T(2,128)S(1)} %get-tuple-element.8.refs_0_, bf16[2,128,64]{2,1,0:T(8,128)(2,1)S(1)} %get-tuple-element.9.refs_1_, bf16[32,48,128]{2,1,0:T(8,128)(2,1)S(1)} %all_to_all.5.refs_2_), custom_call_target="tpu_custom_call" | custom-call | tf_op jit(solution)/shard_map/stack/pallas_call | solution.py:157

commit v3 on v2

--- a/solution.py
+++ b/solution.py
@@ -1,3 +1,5 @@
+import math
+
 import jax
 import jax.numpy as jnp
 from jax import lax
@@ -7,11 +9,17 @@
 
 MAXOFF = 16
 LANES = 128
+OUTER = 4
 F32 = jnp.float32
 BF16 = jnp.bfloat16
 BY_LANES = (((1,), (1,)), ((), ()))
 BY_ROWS = (((0,), (0,)), ((), ()))
 PARAMS = pltpu.CompilerParams(vmem_limit_bytes=24 << 20)
+
+
+def device_at(place, groups):
+    outer = math.gcd(groups, OUTER)
+    return (place % outer) * (groups // outer) + place // outer
 
 
 def on_diagonal(blocks):
@@ -31,7 +39,7 @@
     first = lax.broadcasted_iota(jnp.int32, (slots, slots), 0)
     second = lax.broadcasted_iota(jnp.int32, (slots, slots), 1)
     standing = (first == stations_ref[...]).astype(BF16)
-    wanted = (first == (second % groups) * row_count + second // groups).astype(BF16)
+    wanted = (first == device_at(second % groups, groups) * row_count + second // groups).astype(BF16)
     order = jnp.dot(standing, wanted, preferred_element_type=F32).astype(BF16)
     moves = jnp.dot(offsets_ref[...].astype(BF16), order, preferred_element_type=F32)
     moves_ref[...] = moves.astype(jnp.int32)
@@ -51,13 +59,17 @@
     tmpl_len = templates_ref.shape[2]
     groups = out_ref.shape[0]
     per_tile = LANES // slab
+    places = [0] * groups
+    for place in range(groups):
+        places[device_at(place, groups)] = place
     samples[...] = jnp.zeros_like(samples)
-    out_ref[groups - 1, :MAXOFF] = jnp.zeros((MAXOFF, out_ref.shape[2]), BF16)
+    out_ref[places[groups - 1], :MAXOFF] = jnp.zeros((MAXOFF, out_ref.shape[2]), BF16)
     ones = on_diagonal([jnp.ones(templates_ref.shape[1:], BF16)] * row_count)
     for copy in copies:
         copy.wait()
     samples[:, :length] = traces_ref[...].astype(F32)
     waveforms = on_diagonal([templates_ref[s] for s in range(row_count)])
+    slot_tables(row_count, *held[2:], moves_ref, columns_ref)
     for tile in range(groups * slab // LANES):
         windows = []
         for s in range(row_count):
@@ -76,10 +88,9 @@
         for part in range(per_tile):
             d = tile * per_tile + part
             mine = ncc[LANES - (part + 1) * slab : LANES - part * slab]
-            out_ref[d, MAXOFF:] = mine
+            out_ref[places[d], MAXOFF:] = mine
             if d > 0:
-                out_ref[d - 1, :MAXOFF] = mine[slab - MAXOFF :]
-    slot_tables(row_count, *held[2:], moves_ref, columns_ref)
+                out_ref[places[d - 1], :MAXOFF] = mine[slab - MAXOFF :]
 
 
 def stack_kernel(slab, row_count, moves_ref, weights_ref, parts_ref, out_ref, wide, moved):
@@ -153,7 +164,10 @@
         compiler_params=PARAMS,
         name="correlate",
     )(*(in_hbm(a) for a in sources))
-    received = lax.all_to_all(parts, "tm", split_axis=0, concat_axis=0, tiled=True)
+    order = [device_at(place, groups) for place in range(groups)]
+    received = lax.all_to_all(
+        parts, "tm", split_axis=0, concat_axis=0, axis_index_groups=[order], tiled=True
+    )
     peaks = pl.pallas_call(
         lambda *refs: stack_kernel(slab, row_count, *refs),
         out_shape=jax.ShapeDtypeStruct((slab, tmpl_count), F32),

time: 23.7 us -> 23 us (0.970)
  the two profiles are of different devices: /device:TPU:0 before, /device:TPU:1 now
where the time goes in v3:
time: 23 us; the launch traced here: 22.8 us
  blocking collectives  19.6 us (85%)
  Pallas kernels  3.16 us (14%)
    all_to_all x1, blocking collectives, on_device(): lax.all_to_all(parts, 'tm', split_axis=0, concat_axis=0, axis_index_group...  19.6 us
    pallas_call x1, Pallas kernels, on_device(): pl.pallas_call(lambda *refs: correlate_kernel(slab, *refs), out_shape=(ja...  1.7 us
    pallas_call x1, Pallas kernels, on_device(): pl.pallas_call(lambda *refs: stack_kernel(slab, row_count, *refs), out_sh...  1.46 us

profile of v3, /device:TPU:1, one launch (start us, length us, event | category | flops | bytes accessed | tf_op | source)
XLA Modules:
  0.0 22.8 jit_solution(12309806345286043853)
XLA Ops:
  0.0 1.7 %correlate.1 = (bf16[32,48,128]{2,1,0:T(8,128)(2,1)S(1)}, s32[2,64]{1,0:T(2,128)S(1)}, bf16[2,128,64]{2,1,0:T(8,128)(2,1)S(1)}) custom-call(bf16[2,1151]{1,0:T(2,128)(2,1)} %refs_0_.1, bf16[2,64,128]{2,1,0:T(8,128)(2,1)} %refs_1_.1, s32[1,64]{1,0:T(1,128)} %bitcast.6, s32[2,64]{1,0:T(2,128)} %bitcast.5, bf16[2,64,128]{2,1,0:T(8,128)(2,1)} %bitcast.4), custom_call_target="tpu_custom_call" | custom-call | tf_op jit(solution)/shard_map/correlate/pallas_call | solution.py:150
  1.7 19.6 %all_to_all.5.refs_2_ = bf16[32,48,128]{2,1,0:T(8,128)(2,1)S(1)} all-to-all(bf16[32,48,128]{2,1,0:T(8,128)(2,1)S(1)} %get-tuple-element.10), channel_id=1, replica_groups={{0,8,16,24,1,9,17,25,2,10,18,26,3,11,19,27,4,12,20,28,5,13,21,29,6,14,2..., dimensions={0} | all-to-all | bytes 786432 | tf_op jit(solution)/shard_map/all_to_all | solution.py:168
  21.4 1.5 %stack.1 = f32[32,64]{1,0:T(8,128)} custom-call(s32[2,64]{1,0:T(2,128)S(1)} %get-tuple-element.8.refs_0_, bf16[2,128,64]{2,1,0:T(8,128)(2,1)S(1)} %get-tuple-element.9.refs_1_, bf16[32,48,128]{2,1,0:T(8,128)(2,1)S(1)} %all_to_all.5.refs_2_), custom_call_target="tpu_custom_call" | custom-call | tf_op jit(solution)/shard_map/stack/pallas_call | solution.py:171

commit v4 on v3

--- a/solution.py
+++ b/solution.py
@@ -9,7 +9,8 @@
 
 MAXOFF = 16
 LANES = 128
-OUTER = 4
+OUTER = 16
+STRIDE = 5
 F32 = jnp.float32
 BF16 = jnp.bfloat16
 BY_LANES = (((1,), (1,)), ((), ()))
@@ -19,6 +20,7 @@
 
 def device_at(place, groups):
     outer = math.gcd(groups, OUTER)
+    place = place * (STRIDE if math.gcd(groups, STRIDE) == 1 else 1) % groups
     return (place % outer) * (groups // outer) + place // outer
 
 

time: 23 us -> 22.4 us (0.974)
  blocking collectives: 19.6 us -> 19 us
    all_to_all x1, blocking collectives: 19.6 us -> 19 us  [on_device(): lax.all_to_all(parts, 'tm', split_axis=0, concat_axis=0, axis_index_group...]
where the time goes in v4:
time: 22.4 us; the launch traced here: 22.2 us
  blocking collectives  19 us (85%)
  Pallas kernels  3.16 us (14%)
    all_to_all x1, blocking collectives, on_device(): lax.all_to_all(parts, 'tm', split_axis=0, concat_axis=0, axis_index_group...  19 us
    pallas_call x1, Pallas kernels, on_device(): pl.pallas_call(lambda *refs: correlate_kernel(slab, *refs), out_shape=(ja...  1.7 us
    pallas_call x1, Pallas kernels, on_device(): pl.pallas_call(lambda *refs: stack_kernel(slab, row_count, *refs), out_sh...  1.46 us

profile of v4, /device:TPU:1, one launch (start us, length us, event | category | flops | bytes accessed | tf_op | source)
XLA Modules:
  0.0 22.2 jit_solution(1806664864134801960)
XLA Ops:
  0.0 1.7 %correlate.1 = (bf16[32,48,128]{2,1,0:T(8,128)(2,1)S(1)}, s32[2,64]{1,0:T(2,128)S(1)}, bf16[2,128,64]{2,1,0:T(8,128)(2,1)S(1)}) custom-call(bf16[2,1151]{1,0:T(2,128)(2,1)} %refs_0_.1, bf16[2,64,128]{2,1,0:T(8,128)(2,1)} %refs_1_.1, s32[1,64]{1,0:T(1,128)} %bitcast.6, s32[2,64]{1,0:T(2,128)} %bitcast.5, bf16[2,64,128]{2,1,0:T(8,128)(2,1)} %bitcast.4), custom_call_target="tpu_custom_call" | custom-call | tf_op jit(solution)/shard_map/correlate/pallas_call | solution.py:152
  1.7 19.0 %all_to_all.5.refs_2_ = bf16[32,48,128]{2,1,0:T(8,128)(2,1)S(1)} all-to-all(bf16[32,48,128]{2,1,0:T(8,128)(2,1)S(1)} %get-tuple-element.10), channel_id=1, replica_groups={{0,10,20,30,9,19,29,6,16,26,5,15,25,2,12,22,1,11,21,31,8,18,28,7,17,27,..., dimensions={0} | all-to-all | bytes 786432 | tf_op jit(solution)/shard_map/all_to_all | solution.py:170
  20.8 1.5 %stack.1 = f32[32,64]{1,0:T(8,128)} custom-call(s32[2,64]{1,0:T(2,128)S(1)} %get-tuple-element.8.refs_0_, bf16[2,128,64]{2,1,0:T(8,128)(2,1)S(1)} %get-tuple-element.9.refs_1_, bf16[32,48,128]{2,1,0:T(8,128)(2,1)S(1)} %all_to_all.5.refs_2_), custom_call_target="tpu_custom_call" | custom-call | tf_op jit(solution)/shard_map/stack/pallas_call | solution.py:173

commit v5 on v4

--- a/solution.py
+++ b/solution.py
@@ -39,7 +39,7 @@
     slots = stations_ref.shape[1]
     groups = slots // row_count
     first = lax.broadcasted_iota(jnp.int32, (slots, slots), 0)
-    second = lax.broadcasted_iota(jnp.int32, (slots, slots), 1)
+    second = lax.broadcasted_iota(jnp.int32, (1, slots), 1)
     standing = (first == stations_ref[...]).astype(BF16)
     wanted = (first == device_at(second % groups, groups) * row_count + second // groups).astype(BF16)
     order = jnp.dot(standing, wanted, preferred_element_type=F32).astype(BF16)
@@ -72,13 +72,17 @@
     samples[:, :length] = traces_ref[...].astype(F32)
     waveforms = on_diagonal([templates_ref[s] for s in range(row_count)])
     slot_tables(row_count, *held[2:], moves_ref, columns_ref)
+    row = lax.broadcasted_iota(jnp.int32, (LANES, LANES), 0)
+    lane = lax.broadcasted_iota(jnp.int32, (LANES, LANES), 1)
+
+    def turned(s, tile):
+        stretch = samples[s : s + 1, tile * LANES : (tile + 1) * LANES]
+        return pltpu.roll(jnp.broadcast_to(stretch, (LANES, LANES)), 1, 1, stride=1, stride_axis=0)
+
+    following = [turned(s, 0) for s in range(row_count)]
     for tile in range(groups * slab // LANES):
-        windows = []
-        for s in range(row_count):
-            stretch = samples[s : s + 1, tile * LANES : tile * LANES + LANES + tmpl_len]
-            stretch = jnp.broadcast_to(stretch, (LANES, LANES + tmpl_len))
-            rolled = pltpu.roll(stretch, tmpl_len + 1, 1, stride=1, stride_axis=0)
-            windows.append(rolled[:, :tmpl_len])
+        present, following = following, [turned(s, tile + 1) for s in range(row_count)]
+        windows = [jnp.where(lane <= row, a, b) for a, b in zip(present, following)]
         window = jnp.concatenate(windows, axis=1)
         square = window * window
         high = square.astype(BF16)

time: 22.4 us -> 22.4 us (level)
  no operation moved by 1% of the time
where the time goes in v5:
time: 22.4 us; the launch traced here: 22.2 us
  blocking collectives  19 us (85%)
  Pallas kernels  3.09 us (14%)
    all_to_all x1, blocking collectives, on_device(): lax.all_to_all(parts, 'tm', split_axis=0, concat_axis=0, axis_index_group...  19 us
    pallas_call x1, Pallas kernels, on_device(): pl.pallas_call(lambda *refs: correlate_kernel(slab, *refs), out_shape=(ja...  1.64 us
    pallas_call x1, Pallas kernels, on_device(): pl.pallas_call(lambda *refs: stack_kernel(slab, row_count, *refs), out_sh...  1.46 us

profile of v5, /device:TPU:1, one launch (start us, length us, event | category | flops | bytes accessed | tf_op | source)
XLA Modules:
  0.0 22.2 jit_solution(15950211845333586240)
XLA Ops:
  0.0 1.6 %correlate.1 = (bf16[32,48,128]{2,1,0:T(8,128)(2,1)S(1)}, s32[2,64]{1,0:T(2,128)S(1)}, bf16[2,128,64]{2,1,0:T(8,128)(2,1)S(1)}) custom-call(bf16[2,1151]{1,0:T(2,128)(2,1)} %refs_0_.1, bf16[2,64,128]{2,1,0:T(8,128)(2,1)} %refs_1_.1, s32[1,64]{1,0:T(1,128)} %bitcast.6, s32[2,64]{1,0:T(2,128)} %bitcast.5, bf16[2,64,128]{2,1,0:T(8,128)(2,1)} %bitcast.4), custom_call_target="tpu_custom_call" | custom-call | tf_op jit(solution)/shard_map/correlate/pallas_call | solution.py:156
  1.6 19.0 %all_to_all.5.refs_2_ = bf16[32,48,128]{2,1,0:T(8,128)(2,1)S(1)} all-to-all(bf16[32,48,128]{2,1,0:T(8,128)(2,1)S(1)} %get-tuple-element.10), channel_id=1, replica_groups={{0,10,20,30,9,19,29,6,16,26,5,15,25,2,12,22,1,11,21,31,8,18,28,7,17,27,..., dimensions={0} | all-to-all | bytes 786432 | tf_op jit(solution)/shard_map/all_to_all | solution.py:174
  20.7 1.5 %stack.1 = f32[32,64]{1,0:T(8,128)} custom-call(s32[2,64]{1,0:T(2,128)S(1)} %get-tuple-element.8.refs_0_, bf16[2,128,64]{2,1,0:T(8,128)(2,1)S(1)} %get-tuple-element.9.refs_1_, bf16[32,48,128]{2,1,0:T(8,128)(2,1)S(1)} %all_to_all.5.refs_2_), custom_call_target="tpu_custom_call" | custom-call | tf_op jit(solution)/shard_map/stack/pallas_call | solution.py:177

commit v6 on v5

--- a/solution.py
+++ b/solution.py
@@ -21,7 +21,8 @@
 def device_at(place, groups):
     outer = math.gcd(groups, OUTER)
     place = place * (STRIDE if math.gcd(groups, STRIDE) == 1 else 1) % groups
-    return (place % outer) * (groups // outer) + place // outer
+    device = (place % outer) * (groups // outer) + place // outer
+    return device + 1 - 2 * (device % 2) if groups % 2 == 0 else device
 
 
 def on_diagonal(blocks):

time: 22.4 us -> 22.4 us (level)
  no operation moved by 1% of the time
where the time goes in v6:
time: 22.4 us; the launch traced here: 22.2 us
  blocking collectives  19 us (85%)
  Pallas kernels  3.11 us (14%)
    all_to_all x1, blocking collectives, on_device(): lax.all_to_all(parts, 'tm', split_axis=0, concat_axis=0, axis_index_group...  19 us
    pallas_call x1, Pallas kernels, on_device(): pl.pallas_call(lambda *refs: correlate_kernel(slab, *refs), out_shape=(ja...  1.65 us
    pallas_call x1, Pallas kernels, on_device(): pl.pallas_call(lambda *refs: stack_kernel(slab, row_count, *refs), out_sh...  1.46 us

profile of v6, /device:TPU:1, one launch (start us, length us, event | category | flops | bytes accessed | tf_op | source)
XLA Modules:
  0.0 22.2 jit_solution(12232508648919276899)
XLA Ops:
  0.0 1.6 %correlate.1 = (bf16[32,48,128]{2,1,0:T(8,128)(2,1)S(1)}, s32[2,64]{1,0:T(2,128)S(1)}, bf16[2,128,64]{2,1,0:T(8,128)(2,1)S(1)}) custom-call(bf16[2,1151]{1,0:T(2,128)(2,1)} %refs_0_.1, bf16[2,64,128]{2,1,0:T(8,128)(2,1)} %refs_1_.1, s32[1,64]{1,0:T(1,128)} %bitcast.6, s32[2,64]{1,0:T(2,128)} %bitcast.5, bf16[2,64,128]{2,1,0:T(8,128)(2,1)} %bitcast.4), custom_call_target="tpu_custom_call" | custom-call | tf_op jit(solution)/shard_map/correlate/pallas_call | solution.py:157
  1.7 19.0 %all_to_all.5.refs_2_ = bf16[32,48,128]{2,1,0:T(8,128)(2,1)S(1)} all-to-all(bf16[32,48,128]{2,1,0:T(8,128)(2,1)S(1)} %get-tuple-element.10), channel_id=1, replica_groups={{1,11,21,31,8,18,28,7,17,27,4,14,24,3,13,23,0,10,20,30,9,19,29,6,16,26,..., dimensions={0} | all-to-all | bytes 786432 | tf_op jit(solution)/shard_map/all_to_all | solution.py:175
  20.7 1.5 %stack.1 = f32[32,64]{1,0:T(8,128)} custom-call(s32[2,64]{1,0:T(2,128)S(1)} %get-tuple-element.8.refs_0_, bf16[2,128,64]{2,1,0:T(8,128)(2,1)S(1)} %get-tuple-element.9.refs_1_, bf16[32,48,128]{2,1,0:T(8,128)(2,1)S(1)} %all_to_all.5.refs_2_), custom_call_target="tpu_custom_call" | custom-call | tf_op jit(solution)/shard_map/stack/pallas_call | solution.py:178

commit v7 on v6

--- a/solution.py
+++ b/solution.py
@@ -118,7 +118,7 @@
             moved[b, pl.ds(src, slab, stride=pitch), :] = moment
 
     low_half = lax.broadcasted_iota(jnp.int32, (groups, lanes), 1) < tmpl_count
-    times = 4
+    times = 8
     for q in range(0, slab, times):
         best = None
         for b in range(blocks):

time: 22.4 us -> 22.4 us (level)
  no operation moved by 1% of the time
where the time goes in v7:
time: 22.4 us; the launch traced here: 22.2 us
  blocking collectives  19 us (85%)
  Pallas kernels  3.12 us (14%)
    all_to_all x1, blocking collectives, on_device(): lax.all_to_all(parts, 'tm', split_axis=0, concat_axis=0, axis_index_group...  19 us
    pallas_call x1, Pallas kernels, on_device(): pl.pallas_call(lambda *refs: correlate_kernel(slab, *refs), out_shape=(ja...  1.65 us
    pallas_call x1, Pallas kernels, on_device(): pl.pallas_call(lambda *refs: stack_kernel(slab, row_count, *refs), out_sh...  1.47 us

profile of v7, /device:TPU:1, one launch (start us, length us, event | category | flops | bytes accessed | tf_op | source)
XLA Modules:
  0.0 22.2 jit_solution(15662487895591261160)
XLA Ops:
  0.0 1.6 %correlate.1 = (bf16[32,48,128]{2,1,0:T(8,128)(2,1)S(1)}, s32[2,64]{1,0:T(2,128)S(1)}, bf16[2,128,64]{2,1,0:T(8,128)(2,1)S(1)}) custom-call(bf16[2,1151]{1,0:T(2,128)(2,1)} %refs_0_.1, bf16[2,64,128]{2,1,0:T(8,128)(2,1)} %refs_1_.1, s32[1,64]{1,0:T(1,128)} %bitcast.6, s32[2,64]{1,0:T(2,128)} %bitcast.5, bf16[2,64,128]{2,1,0:T(8,128)(2,1)} %bitcast.4), custom_call_target="tpu_custom_call" | custom-call | tf_op jit(solution)/shard_map/correlate/pallas_call | solution.py:157
  1.7 19.0 %all_to_all.5.refs_2_ = bf16[32,48,128]{2,1,0:T(8,128)(2,1)S(1)} all-to-all(bf16[32,48,128]{2,1,0:T(8,128)(2,1)S(1)} %get-tuple-element.10), channel_id=1, replica_groups={{1,11,21,31,8,18,28,7,17,27,4,14,24,3,13,23,0,10,20,30,9,19,29,6,16,26,..., dimensions={0} | all-to-all | bytes 786432 | tf_op jit(solution)/shard_map/all_to_all | solution.py:175
  20.7 1.5 %stack.1 = f32[32,64]{1,0:T(8,128)} custom-call(s32[2,64]{1,0:T(2,128)S(1)} %get-tuple-element.8.refs_0_, bf16[2,128,64]{2,1,0:T(8,128)(2,1)S(1)} %get-tuple-element.9.refs_1_, bf16[32,48,128]{2,1,0:T(8,128)(2,1)S(1)} %all_to_all.5.refs_2_), custom_call_target="tpu_custom_call" | custom-call | tf_op jit(solution)/shard_map/stack/pallas_call | solution.py:178
